TPU v7x, 32 devices: a whole 2x2x4 slice. The times are simulated.
32 devices in a mesh: seq: 8 (over y, x, core), chan: 4 (over z).
Axes of the slice: x: 2, y: 2, z: 4, core: 2. Of those that a mesh axis runs over, the one named last changes fastest.
Arguments:
- tokens: bfloat16 [2048, 2048], P(('seq', 'chan')), may hold values from -6 to 6
- norm_gain: float32 [2048], replicated, may hold values from 0.1 to 1.9
- entry_projection_matrix: bfloat16 [2, 2048, 4096], P(None, None, 'chan'), may hold values from -0.125 to 0.125
- conv_weight: float32 [4, 4096], P(None, 'chan'), may hold values from -3 to 3
- conv_bias: float32 [4096], P('chan'), may hold values from -3 to 3
- w_x: bfloat16 [4096, 160], P('chan'), may hold values from -0.09375 to 0.09375
- timescale_matrix: bfloat16 [128, 4096], P(None, 'chan'), may hold values from -0.5 to 0.5
- timescale_offset: float32 [4096], P('chan'), may hold values from -8 to -2
- a_log: float32 [16, 4096], P(None, 'chan'), may hold values from -1 to 2.77
- skip_gain: float32 [4096], P('chan'), may hold values from 0.5 to 1.5
- w_out: bfloat16 [4096, 2048], P('chan'), may hold values from -0.09375 to 0.09375
- lengths: int32 [4], replicated, may hold values from 1 to 1024, 1792 in all
- req_order: int32 [4], replicated, may hold values from 0 to 3, each once
Outputs:
- mixed: bfloat16 [2048, 2048], P(('seq', 'chan'))
- last_states: float32 [4, 16, 4096], P(None, None, ('chan', 'seq'))
- conv_edges: bfloat16 [4, 4, 4096], P(None, None, ('chan', 'seq'))
Inputs may be any that keep to these rules, and one draw needn't show every extreme that they name: The lengths sum to exactly 1792, and the longest is exactly 1024. `req_order`: each request appears exactly once.
All inputs are finite; a program needn't handle non-finite values.
Results may differ from a plain program's by a relative error of at most 0.0095.
Values may be sent and summed in bfloat16 or wider, within the bound.
A program may use at most 128 MiB of HBM per device.

v0:
```python
import jax
import jax.numpy as jnp
from jax import lax
from jax.sharding import PartitionSpec as P

STRETCH = 64


def shifted(block, axis, distance):
    devices = range(lax.axis_size(axis))
    route = [(i - distance, i) for i in devices if i - distance in devices]
    return lax.ppermute(block, axis, route)


def sequence_arrangement(lengths, req_order, slot_ids):
    req_count = lengths.shape[0]
    req_index = jnp.arange(req_count, dtype=jnp.int32)
    filled_length_total = (lengths + STRETCH - 1) // STRETCH * STRETCH
    pick_order = (req_order[:, None] == req_index[None, :]).astype(jnp.int32)
    placed_pad = jnp.sum(pick_order * filled_length_total[None, :], axis=1)
    placed_len = jnp.sum(pick_order * lengths[None, :], axis=1)
    end_slots = jnp.cumsum(placed_pad)
    begin_slots = end_slots - placed_pad
    sequence_beginnings = jnp.sum(pick_order * begin_slots[:, None], axis=0)
    inside = (slot_ids[:, None] >= begin_slots[None, :]) & (slot_ids[:, None] < end_slots[None, :])
    slot_owner = jnp.sum(jnp.where(inside, req_index[None, :] + 1, 0), axis=1)
    slot_owner = jnp.where(slot_ids < 0, -1, slot_owner)
    in_request = inside & (slot_ids[:, None] - begin_slots[None, :] < placed_len[None, :])
    present_flag = jnp.sum(jnp.where(in_request, 1, 0), axis=1).astype(jnp.int32)
    return (filled_length_total, sequence_beginnings, slot_owner, present_flag)


def chain_pair(earlier, later):
    return (earlier[0] * later[0], later[0] * earlier[1] + later[1])


def on_device(
    tokens,
    norm_gain,
    entry_projection_matrix,
    conv_weight,
    conv_bias,
    w_x,
    timescale_matrix,
    timescale_offset,
    a_log,
    skip_gain,
    w_out,
    lengths,
    req_order,
):
    tok_rows = tokens.shape[0]
    seq_rows = tok_rows * lax.axis_size("chan")
    chan_width = entry_projection_matrix.shape[2]
    state_size = a_log.shape[0]
    rank_size = timescale_matrix.shape[0]
    halo_count = conv_weight.shape[0] - 1
    req_count = lengths.shape[0]
    base_slot = lax.axis_index("seq") * seq_rows
    ext_slots = base_slot - halo_count + jnp.arange(seq_rows + halo_count, dtype=jnp.int32)
    filled_length_total, sequence_beginnings, padded_request_owner, widened_presence_mask = (
        sequence_arrangement(lengths, req_order, ext_slots)
    )
    slot_owner = padded_request_owner[halo_count:]
    position_presence = widened_presence_mask[halo_count:].astype(jnp.float32)
    widened = tokens.astype(jnp.float32)
    scale_row = lax.rsqrt(jnp.mean(widened * widened, axis=1, keepdims=True) + 1e-05)
    rescaled_entries = (widened * scale_row * norm_gain[None, :]).astype(jnp.bfloat16)
    mapped_signal = jnp.einsum(
        "td,kde->kte",
        lax.all_gather(rescaled_entries, "chan", axis=0, tiled=True),
        entry_projection_matrix,
        preferred_element_type=jnp.float32,
    )
    mixer_signal = (mapped_signal[0] * position_presence[:, None]).astype(jnp.bfloat16)
    switch_signal = mapped_signal[1].astype(jnp.bfloat16)
    rim_rows = shifted(mixer_signal[seq_rows - halo_count :], "seq", 1)
    extended = jnp.concatenate([rim_rows, mixer_signal], axis=0).astype(jnp.float32)
    conv_sum = conv_bias[None, :] + jnp.zeros((seq_rows, chan_width), jnp.float32)
    for shift_by in range(halo_count + 1):
        lower = halo_count - shift_by
        same_req = (padded_request_owner[lower : lower + seq_rows] == slot_owner).astype(
            jnp.float32
        )
        conv_sum = (
            conv_sum
            + conv_weight[lower][None, :] * extended[lower : lower + seq_rows] * same_req[:, None]
        )
    activated = jax.nn.silu(conv_sum).astype(jnp.bfloat16)
    x_proj = lax.psum(jnp.dot(activated, w_x, preferred_element_type=jnp.float32), "chan")
    thin_timescale_factor = x_proj[:, :rank_size].astype(jnp.bfloat16)
    in_coef = x_proj[:, rank_size : rank_size + state_size]
    out_coef = x_proj[:, rank_size + state_size :]
    timescale_values = position_presence[:, None] * jax.nn.softplus(
        jnp.dot(thin_timescale_factor, timescale_matrix, preferred_element_type=jnp.float32)
        + timescale_offset[None, :]
    )
    decay_rate = -jnp.exp(a_log)
    keep_flag = (
        padded_request_owner[halo_count - 1 : halo_count - 1 + seq_rows] == slot_owner
    ).astype(jnp.float32)
    act_wide = activated.astype(jnp.float32)
    block_len = min(16, STRETCH)
    block_count = seq_rows // block_len

    def arrange(values):
        return jnp.swapaxes(values.reshape((block_count, block_len) + values.shape[1:]), 0, 1)

    def advance(running, slot_in):
        state_now, decay_now = running
        step_delta, step_input, step_in, step_out, step_keep = slot_in
        factor = step_keep[:, None, None] * jnp.exp(step_delta[:, None, :] * decay_rate[None])
        state_now = factor * state_now + (step_delta * step_input)[:, None, :] * step_in[:, :, None]
        decay_now = factor * decay_now
        local_out = jnp.sum(step_out[:, :, None] * state_now, axis=1)
        return ((state_now, decay_now), (local_out, step_out[:, :, None] * decay_now))

    empty_state = jnp.zeros((block_count, state_size, chan_width), jnp.float32)
    slot_in = (
        arrange(timescale_values),
        arrange(act_wide),
        arrange(in_coef),
        arrange(out_coef),
        arrange(keep_flag),
    )
    (block_state, block_decay), (local_y, weighted) = lax.scan(
        advance, (empty_state, jnp.ones_like(empty_state)), slot_in
    )
    incl_decay, incl_state = lax.associative_scan(chain_pair, (block_decay, block_state), axis=0)
    own_decay = incl_decay[-1]
    own_state = incl_state[-1]

    def relay(relay_turn, incoming):
        return shifted(own_decay * incoming + own_state, "seq", 1)

    incoming = lax.fori_loop(0, lax.axis_size("seq") - 1, relay, jnp.zeros_like(own_state))
    start_decay = jnp.concatenate([jnp.ones_like(incl_decay[:1]), incl_decay[:-1]], axis=0)
    start_state = jnp.concatenate([jnp.zeros_like(incl_state[:1]), incl_state[:-1]], axis=0)
    begin_state = start_decay * incoming[None] + start_state
    end_state = incl_decay * incoming[None] + incl_state
    carried = jnp.sum(weighted * begin_state[None], axis=2)
    complete_result = (
        jnp.swapaxes(local_y + carried, 0, 1).reshape(seq_rows, chan_width)
        + skip_gain[None, :] * act_wide
    )
    switched_result = (
        position_presence[:, None]
        * complete_result
        * jax.nn.silu(switch_signal.astype(jnp.float32))
    ).astype(jnp.bfloat16)
    summed = lax.psum_scatter(
        jnp.dot(switched_result, w_out, preferred_element_type=jnp.float32),
        "chan",
        scatter_dimension=0,
        tiled=True,
    )
    mixed = (widened + summed).astype(jnp.bfloat16)
    block_ends = base_slot + (jnp.arange(block_count, dtype=jnp.int32) + 1) * block_len - 1
    final_hits = (
        (sequence_beginnings + filled_length_total - 1)[:, None] == block_ends[None, :]
    ).astype(jnp.float32)
    state_part = jnp.einsum("rb,bne->rne", final_hits, end_state, precision=lax.Precision.HIGHEST)
    slots_here = base_slot + jnp.arange(seq_rows, dtype=jnp.int32)
    offsets = jnp.arange(halo_count + 1, dtype=jnp.int32)
    back_pos = lengths[:, None] - (halo_count + 1) + offsets[None, :]
    target = sequence_beginnings[:, None] + back_pos
    picked = (target[:, :, None] == slots_here[None, None, :]) & (back_pos >= 0)[:, :, None]
    pick_matrix = picked.astype(jnp.bfloat16).reshape(req_count * (halo_count + 1), seq_rows)
    edge_part = jnp.dot(pick_matrix, mixer_signal, preferred_element_type=jnp.float32).reshape(
        req_count, halo_count + 1, chan_width
    )
    last_states, edge_sums = (
        lax.psum_scatter(state_part, "seq", scatter_dimension=2, tiled=True),
        lax.psum_scatter(edge_part, "seq", scatter_dimension=2, tiled=True),
    )
    return (mixed, last_states, edge_sums.astype(jnp.bfloat16))


def solution(mesh):
    in_specs = (
        P(("seq", "chan"), None),
        P(),
        P(None, None, "chan"),
        P(None, "chan"),
        P("chan"),
        P("chan", None),
        P(None, "chan"),
        P("chan"),
        P(None, "chan"),
        P("chan"),
        P("chan", None),
        P(),
        P(),
    )
    out_specs = (
        P(("seq", "chan"), None),
        P(None, None, ("chan", "seq")),
        P(None, None, ("chan", "seq")),
    )
    return jax.shard_map(
        on_device, mesh=mesh, in_specs=in_specs, out_specs=out_specs, check_vma=False
    )
```

profile of v0, /device:TPU:0, one launch (start us, length us, event | category | flops | bytes accessed | tf_op | source)
XLA Modules:
  0.0 418.5 jit_solution(2476122839257997157)
XLA Ops:
  17.2 23.8 %all-gather.2.cloned.1.call-done = bf16[256,2048]{1,0:T(8,128)(2,1)} async-done(((bf16[64,2048]{1,0:T(8,128)(2,1)}), bf16[256,2048]{1,0:T(8,128)(2,1)}) %all-gather.2.cloned.1.call-update) | async-done | bytes 1048592 | tf_op jit(solution)/shard_map/all_gather | solution.py:71
  41.0 6.0 %convolution_bitcast_fusion = f32[2,256,1024]{2,1,0:T(8,128)S(1)} fusion(bf16[2,2048,1024]{2,1,0:T(8,128)(2,1)} %param.19, bf16[256,2048]{1,0:T(8,128)(2,1)} %all-gather.2.cloned.1.call-done), kind=kOutput, calls=%fused_computation.16 | convolution fusion | flops 2147483648 | bytes 11534336 | tf_op jit(solution)/shard_map/td,kde->kte/dot_general | solution.py:69
  59.6 3.0 reshape.221
  65.0 27.5 %all-reduce.20.cloned.1.call-done = f32[256,160]{0,1:T(8,128)} async-done(((f32[256,160]{0,1:T(8,128)}), f32[256,160]{0,1:T(8,128)}) %all-reduce.20.cloned.1.call-update) | async-done | bytes 163856 | tf_op jit(solution)/shard_map/psum | solution.py:90
  98.5 94.4 %while.28 = (s32[]{:T(128)}, f32[16,16,1024]{2,1,0:T(8,128)S(1)}, f32[16,16,1024]{2,1,0:T(8,128)S(1)}, f32[16,16,1024]{2,1,0:T(8,128)}, f32[16,16,16,1024]{3,2,1...) while((s32[]{:T(128)}, f32[16,16,1024]{2,1,0:T(8,128)S(1)}, ...), condition=%wide.region_9.10_spmd.clone, body=%wide.region_7.9_spmd.clone.sunk | while | flops 3407875 | bytes 6103448 | solution.py:126
  214.9 3.8 pad.57
  221.7 3.7 pad.65
  232.3 3.5 pad.66
  236.9 5.7 %pad.59 = f32[16,16,1024]{2,1,0:T(8,128)} pad(f32[8,16,1024]{2,1,0:T(8,128)} %add.271, f32[]{:T(128)} %constant.90.clone.1), padding=1_0_1x0_0_0x0_0_0 | pad | bytes 1572868 | tf_op jit(solution)/shard_map/pad | solution.py:129
  244.5 5.7 %pad.58 = f32[16,16,1024]{2,1,0:T(8,128)} pad(f32[8,16,1024]{2,1,0:T(8,128)} %pad_maximum_fusion, f32[]{:T(128)} %constant.90.clone.1), padding=0_1_1x0_0_0x0_0_0 | pad | bytes 1572868 | tf_op jit(solution)/shard_map/pad | solution.py:129
  253.8 35.7 %while.27 = (s32[]{:T(128)}, f32[16,1024]{1,0:T(8,128)S(1)}, f32[16,1024]{1,0:T(8,128)S(1)}, f32[16,1024]{1,0:T(8,128)S(1)}, s32[]{:T(128)}) while((s32[]{:T(128)}, f32[16,1024]{1,0:T(8,128)S(1)}, f32[16,1024]{1,0:T(8,128)S(1)}, f32[16,1024]{1,0:T(8,128)S(1)}, s32[]{:T(128)}) %tuple.80), condition=%wide.region_11.12_spmd, body=%wide.region_10.11_spmd.sunk | while | flops 32770 | bytes 524389 | solution.py:136
  256.0 4.5 %collective-permute-start = (f32[16,1024]{1,0:T(8,128)S(1)}, f32[16,1024]{1,0:T(8,128)S(1)}, u32[]{:S(2)}, u32[]{:S(2)}) collective-permute-start(f32[16,1024]{1,0:T(8,128)S(1)} %multiply_add_fusion.3), channel_id=1, source_target_pairs={{0,4},{4,8},{8,12},{12,16},{16,20},{20,24},{24,28},{1,5},{5,9},{9,... | collective-permute-start | bytes 196616 | tf_op jit(solution)/shard_map/while/body/eval_jaxpr/ppermute | solution.py:12
  261.4 4.7 %collective-permute-start = (f32[16,1024]{1,0:T(8,128)S(1)}, f32[16,1024]{1,0:T(8,128)S(1)}, u32[]{:S(2)}, u32[]{:S(2)}) collective-permute-start(f32[16,1024]{1,0:T(8,128)S(1)} %multiply_add_fusion.3), channel_id=1, source_target_pairs={{0,4},{4,8},{8,12},{12,16},{16,20},{20,24},{24,28},{1,5},{5,9},{9,... | collective-permute-start | bytes 196616 | tf_op jit(solution)/shard_map/while/body/eval_jaxpr/ppermute | solution.py:12
  267.0 4.7 %collective-permute-start = (f32[16,1024]{1,0:T(8,128)S(1)}, f32[16,1024]{1,0:T(8,128)S(1)}, u32[]{:S(2)}, u32[]{:S(2)}) collective-permute-start(f32[16,1024]{1,0:T(8,128)S(1)} %multiply_add_fusion.3), channel_id=1, source_target_pairs={{0,4},{4,8},{8,12},{12,16},{16,20},{20,24},{24,28},{1,5},{5,9},{9,... | collective-permute-start | bytes 196616 | tf_op jit(solution)/shard_map/while/body/eval_jaxpr/ppermute | solution.py:12
  272.6 4.7 %collective-permute-start = (f32[16,1024]{1,0:T(8,128)S(1)}, f32[16,1024]{1,0:T(8,128)S(1)}, u32[]{:S(2)}, u32[]{:S(2)}) collective-permute-start(f32[16,1024]{1,0:T(8,128)S(1)} %multiply_add_fusion.3), channel_id=1, source_target_pairs={{0,4},{4,8},{8,12},{12,16},{16,20},{20,24},{24,28},{1,5},{5,9},{9,... | collective-permute-start | bytes 196616 | tf_op jit(solution)/shard_map/while/body/eval_jaxpr/ppermute | solution.py:12
  278.2 4.7 %collective-permute-start = (f32[16,1024]{1,0:T(8,128)S(1)}, f32[16,1024]{1,0:T(8,128)S(1)}, u32[]{:S(2)}, u32[]{:S(2)}) collective-permute-start(f32[16,1024]{1,0:T(8,128)S(1)} %multiply_add_fusion.3), channel_id=1, source_target_pairs={{0,4},{4,8},{8,12},{12,16},{16,20},{20,24},{24,28},{1,5},{5,9},{9,... | collective-permute-start | bytes 196616 | tf_op jit(solution)/shard_map/while/body/eval_jaxpr/ppermute | solution.py:12
  283.8 4.7 %collective-permute-start = (f32[16,1024]{1,0:T(8,128)S(1)}, f32[16,1024]{1,0:T(8,128)S(1)}, u32[]{:S(2)}, u32[]{:S(2)}) collective-permute-start(f32[16,1024]{1,0:T(8,128)S(1)} %multiply_add_fusion.3), channel_id=1, source_target_pairs={{0,4},{4,8},{8,12},{12,16},{16,20},{20,24},{24,28},{1,5},{5,9},{9,... | collective-permute-start | bytes 196616 | tf_op jit(solution)/shard_map/while/body/eval_jaxpr/ppermute | solution.py:12
  289.4 4.1 multiply_add_fusion.1
  293.6 10.3 %multiply_reduce_fusion.1 = f32[16,16,1024]{2,1,0:T(8,128)S(1)} fusion(f32[16,16,16,1024]{3,2,1,0:T(8,128)} %get-tuple-element.86, f32[16,16,1024]{2,1,0:T(8,128)} %get-tuple-element.232), kind=kLoop, calls=%fused_computation.14 | loop fusion | flops 8126464 | bytes 18874368 | tf_op jit(solution)/shard_map/reduce_sum | solution.py:141
  307.5 5.9 %copy.47 = f32[4,16,1024]{0,1,2:T(8,128)} copy(f32[4,16,1024]{2,0,1:T(4,128)S(1)} %fusion.17) | data formatting | bytes 524288
  313.4 7.1 %reshape.219 = f32[1024,64]{1,0:T(8,128)} reshape(f32[1024,16,4]{2,1,0:T(8,128)} %bitcast.99) | data formatting | bytes 524288
  321.2 3.1 fusion.19
  328.7 35.3 %reduce-scatter.10.cloned.1.call-done = f32[128,64]{1,0:T(8,128)} async-done(((f32[1024,64]{1,0:T(8,128)}), f32[128,64]{1,0:T(8,128)}) %reduce-scatter.10.cloned.1.call-update) | async-done | bytes 32784
  366.5 43.7 %reduce-scatter.8.cloned.1.call-done = f32[64,2048]{1,0:T(8,128)} async-done(((f32[256,2048]{1,0:T(8,128)}), f32[64,2048]{1,0:T(8,128)}) %reduce-scatter.8.cloned.1.call-update) | async-done | bytes 524304 | tf_op jit(solution)/shard_map/reduce_scatter | solution.py:151
  (259 shorter events, 183.6 us)
Async XLA Ops:
  7.2 48.0 %copy-start = (bf16[1024,160]{0,1:T(8,128)(2,1)S(1)}, bf16[1024,160]{0,1:T(8,128)(2,1)}, u32[]{:S(2)}) copy-start(bf16[1024,160]{0,1:T(8,128)(2,1)} %param.22) | copy-start | bytes 983044
  7.2 33.8 %all-gather.2.cloned.1.call-start = ((), (), s32[]{:S(2)}) async-start(), calls=%async_computation.3 | async-start | bytes 1310720 | tf_op jit(solution)/shard_map/all_gather | solution.py:71
  10.2 82.3 %all-reduce.20.cloned.1.call-start = ((), (), s32[]{:S(2)}) async-start(), calls=%async_computation.4 | async-start | bytes 327680 | tf_op jit(solution)/shard_map/psum | solution.py:90
  17.2 36.3 %copy-start.11 = (f32[1024]{0:T(1024)S(1)}, f32[1024]{0:T(1024)}, u32[]{:S(2)}) copy-start(f32[1024]{0:T(1024)} %param.21) | copy-start | bytes 12292
  49.4 3.0 collective-permute-start.1
  56.2 36.3 %copy-start.16 = (f32[1024]{0:T(1024)S(1)}, f32[1024]{0:T(1024)}, u32[]{:S(2)}) copy-start(f32[1024]{0:T(1024)} %param.24) | copy-start | bytes 12292
  56.2 270.8 %reduce-scatter.12.cloned.1.call-start = ((), (), s32[]{:S(2)}) async-start(), calls=%async_computation.7 | async-start | bytes 589824
  62.6 35.9 %copy-start.2 = (f32[16,1024]{1,0:T(8,128)S(1)}, f32[16,1024]{1,0:T(8,128)}, u32[]{:S(2)}) copy-start(f32[16,1024]{1,0:T(8,128)} %exponential_negate_fusion) | copy-start | bytes 196612
  62.6 301.4 %reduce-scatter.10.cloned.1.call-start = ((), (), s32[]{:S(2)}) async-start(), calls=%async_computation.6 | async-start | bytes 589824
  225.4 4.8 %copy-start.4 = (f32[8,16,1024]{2,1,0:T(8,128)S(1)}, f32[8,16,1024]{2,1,0:T(8,128)}, u32[]{:S(2)}) copy-start(f32[8,16,1024]{2,1,0:T(8,128)} %pad.64) | copy-start | bytes 1572868
  225.4 4.8 %copy-start.5 = (f32[8,16,1024]{2,1,0:T(8,128)S(1)}, f32[8,16,1024]{2,1,0:T(8,128)}, u32[]{:S(2)}) copy-start(f32[8,16,1024]{2,1,0:T(8,128)} %pad.65) | copy-start | bytes 1572868
  253.8 2.2 collective-permute-start
  256.0 5.4 %collective-permute-start = (f32[16,1024]{1,0:T(8,128)S(1)}, f32[16,1024]{1,0:T(8,128)S(1)}, u32[]{:S(2)}, u32[]{:S(2)}) collective-permute-start(f32[16,1024]{1,0:T(8,128)S(1)} %multiply_add_fusion.3), channel_id=1, source_target_pairs={{0,4},{4,8},{8,12},{12,16},{16,20},{20,24},{24,28},{1,5},{5,9},{9,... | collective-permute-start | bytes 196616 | tf_op jit(solution)/shard_map/while/body/eval_jaxpr/ppermute | solution.py:12
  261.4 5.6 %collective-permute-start = (f32[16,1024]{1,0:T(8,128)S(1)}, f32[16,1024]{1,0:T(8,128)S(1)}, u32[]{:S(2)}, u32[]{:S(2)}) collective-permute-start(f32[16,1024]{1,0:T(8,128)S(1)} %multiply_add_fusion.3), channel_id=1, source_target_pairs={{0,4},{4,8},{8,12},{12,16},{16,20},{20,24},{24,28},{1,5},{5,9},{9,... | collective-permute-start | bytes 196616 | tf_op jit(solution)/shard_map/while/body/eval_jaxpr/ppermute | solution.py:12
  267.0 5.6 %collective-permute-start = (f32[16,1024]{1,0:T(8,128)S(1)}, f32[16,1024]{1,0:T(8,128)S(1)}, u32[]{:S(2)}, u32[]{:S(2)}) collective-permute-start(f32[16,1024]{1,0:T(8,128)S(1)} %multiply_add_fusion.3), channel_id=1, source_target_pairs={{0,4},{4,8},{8,12},{12,16},{16,20},{20,24},{24,28},{1,5},{5,9},{9,... | collective-permute-start | bytes 196616 | tf_op jit(solution)/shard_map/while/body/eval_jaxpr/ppermute | solution.py:12
  272.6 5.6 %collective-permute-start = (f32[16,1024]{1,0:T(8,128)S(1)}, f32[16,1024]{1,0:T(8,128)S(1)}, u32[]{:S(2)}, u32[]{:S(2)}) collective-permute-start(f32[16,1024]{1,0:T(8,128)S(1)} %multiply_add_fusion.3), channel_id=1, source_target_pairs={{0,4},{4,8},{8,12},{12,16},{16,20},{20,24},{24,28},{1,5},{5,9},{9,... | collective-permute-start | bytes 196616 | tf_op jit(solution)/shard_map/while/body/eval_jaxpr/ppermute | solution.py:12
  278.2 5.6 %collective-permute-start = (f32[16,1024]{1,0:T(8,128)S(1)}, f32[16,1024]{1,0:T(8,128)S(1)}, u32[]{:S(2)}, u32[]{:S(2)}) collective-permute-start(f32[16,1024]{1,0:T(8,128)S(1)} %multiply_add_fusion.3), channel_id=1, source_target_pairs={{0,4},{4,8},{8,12},{12,16},{16,20},{20,24},{24,28},{1,5},{5,9},{9,... | collective-permute-start | bytes 196616 | tf_op jit(solution)/shard_map/while/body/eval_jaxpr/ppermute | solution.py:12
  283.8 5.6 %collective-permute-start = (f32[16,1024]{1,0:T(8,128)S(1)}, f32[16,1024]{1,0:T(8,128)S(1)}, u32[]{:S(2)}, u32[]{:S(2)}) collective-permute-start(f32[16,1024]{1,0:T(8,128)S(1)} %multiply_add_fusion.3), channel_id=1, source_target_pairs={{0,4},{4,8},{8,12},{12,16},{16,20},{20,24},{24,28},{1,5},{5,9},{9,... | collective-permute-start | bytes 196616 | tf_op jit(solution)/shard_map/while/body/eval_jaxpr/ppermute | solution.py:12
  293.6 11.7 %copy-start.13 = (s32[4]{0:T(128)S(1)}, s32[4]{0:T(128)}, u32[]{:S(2)}) copy-start(s32[4]{0:T(128)} %add_add_fusion.1) | copy-start | bytes 52
  293.6 11.7 %copy-start.14 = (s32[16]{0:T(128)S(1)}, s32[16]{0:T(128)}, u32[]{:S(2)}) copy-start(s32[16]{0:T(128)} %add_add_fusion) | copy-start | bytes 196
  313.4 7.8 %copy-start.12 = (f32[1024]{0:T(1024)S(1)}, f32[1024]{0:T(1024)}, u32[]{:S(2)}) copy-start(f32[1024]{0:T(1024)} %param.26) | copy-start | bytes 12292
  321.1 89.1 %reduce-scatter.8.cloned.1.call-start = ((), (), s32[]{:S(2)}) async-start(), calls=%async_computation.5 | async-start | bytes 2621440 | tf_op jit(solution)/shard_map/reduce_scatter | solution.py:151
  324.3 85.9 %copy-start.9 = (bf16[64,2048]{1,0:T(8,128)(2,1)S(1)}, bf16[64,2048]{1,0:T(8,128)(2,1)}, u32[]{:S(2)}) copy-start(bf16[64,2048]{1,0:T(8,128)(2,1)} %param.17) | copy-start | bytes 786436
  324.4 87.6 %copy-start.1 = (bf16[1024,160]{0,1:T(8,128)(2,1)S(1)}, bf16[1024,160]{0,1:T(8,128)(2,1)}, u32[]{:S(2)}) copy-start(bf16[1024,160]{0,1:T(8,128)(2,1)} %param.22) | copy-start | bytes 983044
  (6 other events, 11.5 us)
Sparse Core Ops, SparseCore 0:
  10.3 30.6 all-gather.1
  56.3 36.1 all-reduce.19
  95.9 33.8 reduce-scatter.11
  321.2 42.7 reduce-scatter.9
  366.3 43.8 reduce-scatter.7
where the time goes:
time: 424 us; the launch traced here: 419 us
  waiting for transfers between devices  137 us (32%)
  local copies, waits for them, and re-layouts  115 us (27%)
  other arithmetic  106 us (25%)
  starting transfers between devices  31.1 us (7%)
  matrix products  15.2 us (4%)
  between operations  14.1 us (3%)
    reduce_scatter x1, waiting for transfers between devices, on_device(): lax.psum_scatter(jnp.dot(switched_result, w_out, preferred_element_type=j...  43.7 us
    unnamed x7, waiting for transfers between devices  35.4 us
    pad x12, local copies, waits for them, and re-layouts, on_device(): lax.associative_scan(chain_pair, (block_decay, block_state), axis=0)  34.3 us
    ppermute x8, starting transfers between devices, shifted(): return lax.ppermute(block, axis, route)  30.9 us
    psum x1, waiting for transfers between devices, on_device(): lax.psum(jnp.dot(activated, w_x, preferred_element_type=jnp.float32), 'ch...  27.5 us
    unnamed x43, local copies, waits for them, and re-layouts  25.6 us
    all_gather x1, waiting for transfers between devices, on_device(): lax.all_gather(rescaled_entries, 'chan', axis=0, tiled=True)  23.8 us
    dynamic_update_slice x16, other arithmetic, on_device(): lax.scan(advance, (empty_state, jnp.ones_like(empty_state)), slot_in)  23.4 us
  transfers between devices with their start and end apart: 13, of which 11 were waited for; matrix products, arithmetic and copies ran while one was open for 52% of the time, Pallas kernels for 0%

commit v1 on v0

--- a/solution.py
+++ b/solution.py
@@ -1,6 +1,8 @@
 import jax
 import jax.numpy as jnp
 from jax import lax
+from jax.experimental import pallas as pl
+from jax.experimental.pallas import tpu as pltpu
 from jax.sharding import PartitionSpec as P
 
 STRETCH = 64
@@ -30,8 +32,158 @@
     return (filled_length_total, sequence_beginnings, slot_owner, present_flag)
 
 
-def chain_pair(earlier, later):
-    return (earlier[0] * later[0], later[0] * earlier[1] + later[1])
+def exchange(arrays, plans, collective_id):
+    count = len(arrays)
+    sizes = [lax.axis_size(axis) for axis, _ in plans]
+    axes = list(dict.fromkeys(axis for axis, _ in plans))
+
+    def kernel(*refs):
+        ins, outs = refs[:count], refs[count : 2 * count]
+        send_sems, recv_sems = refs[2 * count : 3 * count], refs[3 * count : 4 * count]
+        own_sems = refs[4 * count]
+        barrier = pltpu.get_barrier_semaphore()
+        greeted = 0
+        for axis in axes:
+            n = lax.axis_size(axis)
+            me = lax.axis_index(axis)
+            for step in range(1, n):
+                pl.semaphore_signal(
+                    barrier,
+                    inc=1,
+                    device_id={axis: lax.rem(me + step, n)},
+                    device_id_type=pl.DeviceIdType.MESH,
+                )
+            greeted += n - 1
+        pl.semaphore_wait(barrier, greeted)
+        copies = []
+        for i, (axis, mode) in enumerate(plans):
+            n = sizes[i]
+            me = lax.axis_index(axis)
+            for step in range(1, n):
+                peer = lax.rem(me + step, n)
+                copies.append(
+                    pltpu.make_async_remote_copy(
+                        src_ref=ins[i] if mode == "gather" else ins[i].at[peer],
+                        dst_ref=outs[i].at[me],
+                        send_sem=send_sems[i].at[step - 1],
+                        recv_sem=recv_sems[i].at[step - 1],
+                        device_id={axis: peer},
+                        device_id_type=pl.DeviceIdType.MESH,
+                    )
+                )
+                copies[-1].start()
+        for i, (axis, mode) in enumerate(plans):
+            me = lax.axis_index(axis)
+            copies.append(
+                pltpu.make_async_copy(
+                    ins[i] if mode == "gather" else ins[i].at[me], outs[i].at[me], own_sems.at[i]
+                )
+            )
+            copies[-1].start()
+        for copy in copies:
+            copy.wait()
+
+    out_shape = [
+        jax.ShapeDtypeStruct(
+            ((n,) + x.shape) if mode == "gather" else x.shape, x.dtype
+        )
+        for x, n, (_, mode) in zip(arrays, sizes, plans)
+    ]
+    sems = [pltpu.SemaphoreType.DMA((n - 1,)) for n in sizes]
+    return pl.pallas_call(
+        kernel,
+        out_shape=out_shape,
+        in_specs=[pl.BlockSpec(memory_space=pl.ANY)] * count,
+        out_specs=[pl.BlockSpec(memory_space=pl.ANY)] * count,
+        scratch_shapes=sems + sems + [pltpu.SemaphoreType.DMA((count,))],
+        compiler_params=pltpu.CompilerParams(collective_id=collective_id, has_side_effects=True),
+    )(*arrays)
+
+
+LANES = 128
+GROUP = 8
+
+
+def run_scan(delta, drive, rate, in_wide, keep, out_wide=None, begin=None):
+    rows, width = delta.shape
+    state_size = rate.shape[0]
+    tiles = width // LANES
+    stretches = rows // STRETCH
+    full = out_wide is not None
+
+    def kernel(*refs):
+        if full:
+            keep_ref, delta_ref, drive_ref, rate_ref, in_ref, out_ref, begin_ref, y_ref, end_ref = refs
+        else:
+            keep_ref, delta_ref, drive_ref, rate_ref, in_ref, end_ref = refs
+        spans = [pl.ds(l * LANES, LANES) for l in range(tiles)]
+
+        def group(g, carry):
+            states, totals = carry
+            states, totals = list(states), list(totals)
+            first = pl.multiple_of(g * GROUP, GROUP)
+            rates = [rate_ref[:, span] for span in spans]
+            deltas = [delta_ref[pl.ds(first, GROUP), span] for span in spans]
+            drives = [drive_ref[pl.ds(first, GROUP), span] for span in spans]
+            if not full:
+                totals = [t + d for t, d in zip(totals, deltas)]
+            ys = [[] for _ in spans]
+            for j in range(GROUP):
+                b = in_ref[first + j]
+                c = out_ref[first + j] if full else None
+                for l in range(tiles):
+                    factor = jnp.exp(deltas[l][j : j + 1] * rates[l])
+                    states[l] = factor * states[l] + drives[l][j : j + 1] * b
+                    if full:
+                        ys[l].append(jnp.sum(c * states[l], axis=0, keepdims=True))
+            if full:
+                for l in range(tiles):
+                    y_ref[pl.ds(first, GROUP), spans[l]] = jnp.concatenate(ys[l], axis=0)
+            return tuple(states), tuple(totals)
+
+        def stretch(s, carry):
+            states, totals = carry
+            states = tuple(keep_ref[s] * state for state in states)
+            per = STRETCH // GROUP
+            states, totals = lax.fori_loop(s * per, (s + 1) * per, group, (states, totals))
+            if full:
+                for l in range(tiles):
+                    end_ref[s, :, spans[l]] = states[l]
+            return states, totals
+
+        if full:
+            states = tuple(begin_ref[:, span] for span in spans)
+            totals = ()
+        else:
+            states = tuple(jnp.zeros((state_size, LANES), jnp.float32) for _ in spans)
+            totals = tuple(jnp.zeros((GROUP, LANES), jnp.float32) for _ in spans)
+        states, totals = lax.fori_loop(0, stretches, stretch, (states, totals))
+        if not full:
+            for l in range(tiles):
+                end_ref[pl.ds(0, state_size), spans[l]] = states[l]
+                end_ref[pl.ds(state_size, GROUP), spans[l]] = totals[l]
+
+    vmem = pl.BlockSpec(memory_space=pltpu.VMEM)
+    smem = pl.BlockSpec(memory_space=pltpu.SMEM)
+    f32 = jnp.float32
+    if full:
+        operands = (keep, delta, drive, rate, in_wide, out_wide, begin)
+        out_shape = (
+            jax.ShapeDtypeStruct((rows, width), f32),
+            jax.ShapeDtypeStruct((stretches, state_size, width), f32),
+        )
+        out_specs = (vmem, vmem)
+    else:
+        operands = (keep, delta, drive, rate, in_wide)
+        out_shape = jax.ShapeDtypeStruct((state_size + GROUP, width), f32)
+        out_specs = vmem
+    return pl.pallas_call(
+        kernel,
+        out_shape=out_shape,
+        in_specs=[smem] + [vmem] * (len(operands) - 1),
+        out_specs=out_specs,
+        compiler_params=pltpu.CompilerParams(vmem_limit_bytes=40 * 1024 * 1024),
+    )(*operands)
 
 
 def on_device(
@@ -68,7 +220,7 @@
     rescaled_entries = (widened * scale_row * norm_gain[None, :]).astype(jnp.bfloat16)
     mapped_signal = jnp.einsum(
         "td,kde->kte",
-        lax.all_gather(rescaled_entries, "chan", axis=0, tiled=True),
+        exchange([rescaled_entries], [("chan", "gather")], 0)[0].reshape(seq_rows, -1),
         entry_projection_matrix,
         preferred_element_type=jnp.float32,
     )
@@ -87,7 +239,8 @@
             + conv_weight[lower][None, :] * extended[lower : lower + seq_rows] * same_req[:, None]
         )
     activated = jax.nn.silu(conv_sum).astype(jnp.bfloat16)
-    x_proj = lax.psum(jnp.dot(activated, w_x, preferred_element_type=jnp.float32), "chan")
+    x_part = jnp.dot(activated, w_x, preferred_element_type=jnp.float32)
+    x_proj = jnp.sum(exchange([x_part], [("chan", "gather")], 1)[0], axis=0)
     thin_timescale_factor = x_proj[:, :rank_size].astype(jnp.bfloat16)
     in_coef = x_proj[:, rank_size : rank_size + state_size]
     out_coef = x_proj[:, rank_size + state_size :]
@@ -96,70 +249,45 @@
         + timescale_offset[None, :]
     )
     decay_rate = -jnp.exp(a_log)
-    keep_flag = (
-        padded_request_owner[halo_count - 1 : halo_count - 1 + seq_rows] == slot_owner
-    ).astype(jnp.float32)
     act_wide = activated.astype(jnp.float32)
-    block_len = min(16, STRETCH)
+    span_count = lax.axis_size("seq")
+    me = lax.axis_index("seq")
+    block_len = STRETCH
     block_count = seq_rows // block_len
-
-    def arrange(values):
-        return jnp.swapaxes(values.reshape((block_count, block_len) + values.shape[1:]), 0, 1)
-
-    def advance(running, slot_in):
-        state_now, decay_now = running
-        step_delta, step_input, step_in, step_out, step_keep = slot_in
-        factor = step_keep[:, None, None] * jnp.exp(step_delta[:, None, :] * decay_rate[None])
-        state_now = factor * state_now + (step_delta * step_input)[:, None, :] * step_in[:, :, None]
-        decay_now = factor * decay_now
-        local_out = jnp.sum(step_out[:, :, None] * state_now, axis=1)
-        return ((state_now, decay_now), (local_out, step_out[:, :, None] * decay_now))
-
-    empty_state = jnp.zeros((block_count, state_size, chan_width), jnp.float32)
-    slot_in = (
-        arrange(timescale_values),
-        arrange(act_wide),
-        arrange(in_coef),
-        arrange(out_coef),
-        arrange(keep_flag),
-    )
-    (block_state, block_decay), (local_y, weighted) = lax.scan(
-        advance, (empty_state, jnp.ones_like(empty_state)), slot_in
-    )
-    incl_decay, incl_state = lax.associative_scan(chain_pair, (block_decay, block_state), axis=0)
-    own_decay = incl_decay[-1]
-    own_state = incl_state[-1]
-
-    def relay(relay_turn, incoming):
-        return shifted(own_decay * incoming + own_state, "seq", 1)
-
-    incoming = lax.fori_loop(0, lax.axis_size("seq") - 1, relay, jnp.zeros_like(own_state))
-    start_decay = jnp.concatenate([jnp.ones_like(incl_decay[:1]), incl_decay[:-1]], axis=0)
-    start_state = jnp.concatenate([jnp.zeros_like(incl_state[:1]), incl_state[:-1]], axis=0)
-    begin_state = start_decay * incoming[None] + start_state
-    end_state = incl_decay * incoming[None] + incl_state
-    carried = jnp.sum(weighted * begin_state[None], axis=2)
-    complete_result = (
-        jnp.swapaxes(local_y + carried, 0, 1).reshape(seq_rows, chan_width)
-        + skip_gain[None, :] * act_wide
-    )
+    heads = jnp.arange(span_count * block_count, dtype=jnp.int32) * block_len
+    _, _, edge_owner, _ = sequence_arrangement(
+        lengths, req_order, jnp.concatenate([heads - 1, heads])
+    )
+    keep_all = (edge_owner[: heads.shape[0]] == edge_owner[heads.shape[0] :]).astype(jnp.float32)
+    keep_all = keep_all.reshape(span_count, block_count)
+    mine = (jnp.arange(span_count) == me).astype(jnp.float32)
+    keep_here = jnp.sum(keep_all * mine[:, None], axis=0)
+    drive = timescale_values * act_wide
+    in_wide = jnp.broadcast_to(in_coef[:, :, None], in_coef.shape + (LANES,))
+    out_wide = jnp.broadcast_to(out_coef[:, :, None], out_coef.shape + (LANES,))
+    span_end = run_scan(timescale_values, drive, decay_rate, in_wide, keep_here)
+    span_ends = exchange([span_end], [("seq", "gather")], 2)[0]
+    incoming = jnp.zeros((state_size, chan_width), jnp.float32)
+    for span in range(span_count - 1):
+        total = jnp.sum(span_ends[span, state_size:], axis=0, keepdims=True)
+        onward = jnp.min(keep_all[span]) * jnp.exp(total * decay_rate) * incoming
+        incoming = jnp.where(span < me, onward + span_ends[span, :state_size], incoming)
+    scanned, end_state = run_scan(
+        timescale_values, drive, decay_rate, in_wide, keep_here, out_wide, incoming
+    )
+    complete_result = scanned + skip_gain[None, :] * act_wide
     switched_result = (
         position_presence[:, None]
         * complete_result
         * jax.nn.silu(switch_signal.astype(jnp.float32))
     ).astype(jnp.bfloat16)
-    summed = lax.psum_scatter(
-        jnp.dot(switched_result, w_out, preferred_element_type=jnp.float32),
-        "chan",
-        scatter_dimension=0,
-        tiled=True,
-    )
-    mixed = (widened + summed).astype(jnp.bfloat16)
+    out_part = jnp.dot(switched_result, w_out, preferred_element_type=jnp.float32)
+    out_part = out_part.astype(jnp.bfloat16).reshape(-1, tok_rows, w_out.shape[1])
     block_ends = base_slot + (jnp.arange(block_count, dtype=jnp.int32) + 1) * block_len - 1
     final_hits = (
         (sequence_beginnings + filled_length_total - 1)[:, None] == block_ends[None, :]
     ).astype(jnp.float32)
-    state_part = jnp.einsum("rb,bne->rne", final_hits, end_state, precision=lax.Precision.HIGHEST)
+    state_part = jnp.sum(final_hits[:, :, None, None] * end_state[None], axis=1)
     slots_here = base_slot + jnp.arange(seq_rows, dtype=jnp.int32)
     offsets = jnp.arange(halo_count + 1, dtype=jnp.int32)
     back_pos = lengths[:, None] - (halo_count + 1) + offsets[None, :]
@@ -169,11 +297,15 @@
     edge_part = jnp.dot(pick_matrix, mixer_signal, preferred_element_type=jnp.float32).reshape(
         req_count, halo_count + 1, chan_width
     )
-    last_states, edge_sums = (
-        lax.psum_scatter(state_part, "seq", scatter_dimension=2, tiled=True),
-        lax.psum_scatter(edge_part, "seq", scatter_dimension=2, tiled=True),
-    )
-    return (mixed, last_states, edge_sums.astype(jnp.bfloat16))
+    tails = jnp.concatenate([state_part, edge_part], axis=1)
+    tails = tails.reshape(-1, span_count, chan_width // span_count)
+    out_blocks, tail_blocks = exchange(
+        [out_part, jnp.swapaxes(tails, 0, 1)], [("chan", "scatter"), ("seq", "scatter")], 3
+    )
+    summed = jnp.sum(out_blocks.astype(jnp.float32), axis=0)
+    mixed = (widened + summed).astype(jnp.bfloat16)
+    tail = jnp.sum(tail_blocks, axis=0).reshape(req_count, -1, chan_width // span_count)
+    return (mixed, tail[:, :state_size], tail[:, state_size:].astype(jnp.bfloat16))
 
 
 def solution(mesh):

time: 424 us -> 149 us (0.35)
  the two profiles are of different devices: /device:TPU:0 before, /device:TPU:9 now
where the time goes in v1:
time: 149 us; the launch traced here: 148 us
  Pallas kernels  103 us (69%)
  other arithmetic  19.7 us (13%)
  matrix products  13.8 us (9%)
  local copies, waits for them, and re-layouts  7.64 us (5%)
  starting transfers between devices  3.5 us (2%)
    pallas_call x4, Pallas kernels, exchange(): pl.pallas_call(kernel, out_shape=out_shape, in_specs=[pl.BlockSpec(memory...  91.5 us
    pallas_call x2, Pallas kernels, run_scan(): pl.pallas_call(kernel, out_shape=out_shape, in_specs=[smem] + [vmem] * (l...  11.2 us
    dot_general x1, matrix products, on_device(): jnp.einsum('td,kde->kte', exchange([rescaled_entries], [('chan', 'gather'...  6.07 us
    select_n x1, other arithmetic, on_device(): jnp.where(span < me, onward + span_ends[span, :state_size], incoming)  5.68 us
    dot_general x1, matrix products, on_device(): jnp.dot(switched_result, w_out, preferred_element_type=jnp.float32)  4.98 us
    ppermute x1, starting transfers between devices, shifted(): return lax.ppermute(block, axis, route)  3.5 us
  transfers between devices with their start and end apart: 1, of which 0 were waited for; matrix products, arithmetic and copies ran while one was open for 2% of the time, Pallas kernels for 0%

profile of v1, /device:TPU:9, one launch (start us, length us, event | category | flops | bytes accessed | tf_op | source)
XLA Modules:
  0.0 148.5 jit_solution(4169146573355992028)
XLA Ops:
  1.4 0.8 select_reduce_fusion.6
  2.4 0.9 select_reduce_fusion.3
  3.4 1.1 fusion.16
  4.5 1.8 %fusion.18.refs_0_ = bf16[64,2048]{1,0:T(8,128)(2,1)} fusion(bf16[64,2048]{1,0:T(8,128)(2,1)} %param.13, f32[2048]{0:T(1024)} %param.14, f32[64]{0:T(128)S(1)} %add_rsqrt_fusion), kind=kLoop, calls=%fused_computation.40 | loop fusion | flops 524288 | bytes 532736 | tf_op jit(solution)/shard_map/convert_element_type | solution.py:220
  6.3 26.5 %shard_map.148 = bf16[4,64,2048]{2,1,0:T(8,128)(2,1)} custom-call(bf16[64,2048]{1,0:T(8,128)(2,1)} %fusion.18.refs_0_), custom_call_target="tpu_custom_call" | custom-call | tf_op jit(solution)/shard_map/pallas_call | solution.py:93
  32.9 6.1 %convolution_bitcast_fusion = f32[2,256,1024]{2,1,0:T(8,128)S(1)} fusion(bf16[256,2048,1]{1,0,2:T(8,128)(2,1)} %bitcast.77, bf16[2,2048,1024]{2,1,0:T(8,128)(2,1)} %param.15), kind=kOutput, calls=%fused_computation.3 | convolution fusion | flops 2147483648 | bytes 11534336 | tf_op jit(solution)/shard_map/td,kde->kte/dot_general | solution.py:221
  39.1 3.5 %collective-permute-start = (bf16[3,1024]{1,0:T(4,128)(2,1)S(1)}, bf16[3,1024]{1,0:T(4,128)(2,1)S(1)}, u32[]{:S(2)}, u32[]{:S(2)}) collective-permute-start(bf16[3,1024]{1,0:T(4,128)(2,1)S(1)} %slice.202), channel_id=1, source_target_pairs={{0,4},{4,8},{8,12},{12,16},{16,20},{20,24},{24,28},{1,5},{5,9},{9,... | collective-permute-start | bytes 18440 | tf_op jit(solution)/shard_map/ppermute | solution.py:14
  43.7 0.9 fusion.21
  45.5 0.9 multiply_convert_fusion.1
  46.4 1.0 fusion.48.refs_0_
  47.5 25.1 %shard_map.149 = f32[4,256,160]{2,1,0:T(8,128)} custom-call(f32[256,160]{1,0:T(8,128)} %fusion.48.refs_0_), custom_call_target="tpu_custom_call" | custom-call | tf_op jit(solution)/shard_map/pallas_call | solution.py:93
  72.5 1.3 reduce_sum.185
  74.6 0.9 convert_multiply_fusion.2
  76.5 4.2 %shard_map.150.refs_0_ = f32[24,1024]{1,0:T(8,128)S(1)} custom-call(f32[4]{0:T(128)S(1)} %select_reduce_fusion.2.refs_0_, f32[256,1024]{1,0:T(8,128)S(1)} %get-tuple-element.41.refs_1_, f32[256,1024]{1,0:T(8,128)S(1)} %get-tuple-element.40.refs_2_, f32[16,1024]{1,0:T(8,128)S(1)} %exponential_negate_fusion.refs_3_, f32[256,16,128]{2,1,0:T(8,128)S(1)} %broadcast_in_dim.48.refs_4_), custom_call_target="tpu_custom_call" | custom-call | tf_op jit(solution)/shard_map/pallas_call | solution.py:180
  81.3 14.0 %shard_map.151 = f32[8,24,1024]{2,1,0:T(8,128)} custom-call(f32[24,1024]{1,0:T(8,128)} %copy-done.3), custom_call_target="tpu_custom_call" | custom-call | tf_op jit(solution)/shard_map/pallas_call | solution.py:93
  95.4 1.0 slice_reduce_fusion.6
  96.4 5.7 %fusion.29.refs_6_ = f32[16,1024]{1,0:T(8,128)S(1)} fusion(f32[8,24,1024]{2,1,0:T(8,128)} %shard_map.151, f32[1024]{0:T(1024)S(1)} %get-tuple-element.12, f32[]{:T(128)} %get-tuple-element.23, f32[1024]{0:T(1024)S(1)} %get-tuple-element.13, f32[]{:T(128)} %get-tuple-element.24, f32[1024]{0:T(1024)S(1)} %get-tuple-element.14, f32[]{:T(128)} %get-tuple-element.25, ...), kind=kLoop, calls=%fused_computation.53 | loop fusion | flops 589824 | bytes 618531 | tf_op jit(solution)/shard_map/jit(_where)/select_n | solution.py:274
  102.1 1.5 %broadcast_in_dim.49.refs_5_ = f32[256,16,128]{2,1,0:T(8,128)S(1)} broadcast(f32[256,16]{1,0:T(8,128)} %get-tuple-element.29), dimensions={0,1} | broadcast | bytes 2113536 | tf_op jit(solution)/shard_map/broadcast_in_dim | solution.py:267
  103.6 7.0 %shard_map.152 = (f32[256,1024]{1,0:T(8,128)S(1)}, f32[4,16,1024]{2,1,0:T(8,128)S(1)}) custom-call(f32[4]{0:T(128)S(1)} %select_reduce_fusion.2.refs_0_, f32[256,1024]{1,0:T(8,128)S(1)} %copy-done.2, f32[256,1024]{1,0:T(8,128)S(1)} %get-tuple-element.40.refs_2_, f32[16,1024]{1,0:T(8,128)S(1)} %exponential_negate_fusion.refs_3_, ...), custom_call_target="tpu_custom_call" | custom-call | tf_op jit(solution)/shard_map/pallas_call | solution.py:180
  110.7 1.0 copy-done.4
  113.2 5.0 %convolution_convert_fusion = bf16[256,2048]{1,0:T(8,128)(2,1)} fusion(bf16[1024,2048]{1,0:T(8,128)(2,1)} %param.23, f32[256,1024]{1,0:T(8,128)S(1)} %copy-done.5, bf16[256,1024]{1,0:T(8,128)(2,1)S(1)} %copy-done.9, f32[2,256,1024]{2,1,0:T(8,128)} %copy-done.7, f32[1024]{0:T(1024)S(1)} %copy-done.16, f32[256]{0:T(256)S(1)} %slice_convert_fusion.4), kind=kOutput, calls=%fused_computation.1 | convolution fusion | flops 1077149696 | bytes 7345152 | tf_op jit(solution)/shard_map/dot_general | solution.py:284
  118.1 25.9 %shard_map.153 = (bf16[4,64,2048]{2,1,0:T(8,128)(2,1)}, f32[8,80,128]{2,1,0:T(8,128)}) custom-call(bf16[4,64,2048]{2,1,0:T(8,128)(2,1)} %bitcast.78, f32[8,80,128]{2,1,0:T(8,128)} %bitcast.76), custom_call_target="tpu_custom_call" | custom-call | tf_op jit(solution)/shard_map/pallas_call | solution.py:93
  144.1 1.0 reduce_sum.196
  146.3 1.4 convert_reduce_fusion
  (77 shorter events, 9.0 us)
Async XLA Ops:
  0.6 45.8 %copy-start = (bf16[1024,160]{0,1:T(8,128)(2,1)S(1)}, bf16[1024,160]{0,1:T(8,128)(2,1)}, u32[]{:S(2)}) copy-start(bf16[1024,160]{0,1:T(8,128)(2,1)} %param.18) | copy-start | bytes 983044
  32.9 10.4 %copy-start.12 = (f32[4,1024]{1,0:T(4,128)S(1)}, f32[4,1024]{1,0:T(4,128)}, u32[]{:S(2)}) copy-start(f32[4,1024]{1,0:T(4,128)} %param.16) | copy-start | bytes 49156
  32.9 10.6 %copy-start.10 = (f32[16,1024]{1,0:T(8,128)S(1)}, f32[16,1024]{1,0:T(8,128)}, u32[]{:S(2)}) copy-start(f32[16,1024]{1,0:T(8,128)} %param.21) | copy-start | bytes 196612
  39.0 6.5 %copy-start.7 = (f32[2,256,1024]{2,1,0:T(8,128)}, f32[2,256,1024]{2,1,0:T(8,128)S(1)}, u32[]{:S(2)}) copy-start(f32[2,256,1024]{2,1,0:T(8,128)S(1)} %convolution_bitcast_fusion) | copy-start | bytes 6291460
  39.0 6.5 %copy-start.13 = (f32[1024]{0:T(1024)S(1)}, f32[1024]{0:T(1024)}, u32[]{:S(2)}) copy-start(f32[1024]{0:T(1024)} %param.17) | copy-start | bytes 12292
  39.1 6.2 %collective-permute-start = (bf16[3,1024]{1,0:T(4,128)(2,1)S(1)}, bf16[3,1024]{1,0:T(4,128)(2,1)S(1)}, u32[]{:S(2)}, u32[]{:S(2)}) collective-permute-start(bf16[3,1024]{1,0:T(4,128)(2,1)S(1)} %slice.202), channel_id=1, source_target_pairs={{0,4},{4,8},{8,12},{12,16},{16,20},{20,24},{24,28},{1,5},{5,9},{9,... | collective-permute-start | bytes 18440 | tf_op jit(solution)/shard_map/ppermute | solution.py:14
  46.4 28.2 %copy-start.8 = (bf16[256,1024]{1,0:T(8,128)(2,1)}, bf16[256,1024]{1,0:T(8,128)(2,1)S(1)}, u32[]{:S(2)}) copy-start(bf16[256,1024]{1,0:T(8,128)(2,1)S(1)} %multiply_convert_fusion.1) | copy-start | bytes 1572868
  46.4 28.2 %copy-start.14 = (bf16[128,1024]{1,0:T(8,128)(2,1)S(1)}, bf16[128,1024]{1,0:T(8,128)(2,1)}, u32[]{:S(2)}) copy-start(bf16[128,1024]{1,0:T(8,128)(2,1)} %param.19) | copy-start | bytes 786436
  46.4 28.2 %copy-start.15 = (f32[1024]{0:T(1024)S(1)}, f32[1024]{0:T(1024)}, u32[]{:S(2)}) copy-start(f32[1024]{0:T(1024)} %param.20) | copy-start | bytes 12292
  75.5 1.0 copy-start.1
  80.7 0.6 copy-start.3
  95.4 8.2 %copy-start.2 = (f32[256,1024]{1,0:T(8,128)S(1)}, f32[256,1024]{1,0:T(8,128)}, u32[]{:S(2)}) copy-start(f32[256,1024]{1,0:T(8,128)} %copy-done.1) | copy-start | bytes 3145732
  103.6 8.2 %copy-start.11 = (f32[4,4,1024]{2,1,0:T(4,128)S(1)}, f32[4,4,1024]{2,1,0:T(4,128)}, u32[]{:S(2)}) copy-start(f32[4,4,1024]{2,1,0:T(4,128)} %fusion.21) | copy-start | bytes 196612
  110.6 1.0 copy-start.4
  111.6 1.0 copy-start.9
  111.6 1.0 copy-start.16
  111.6 1.5 %copy-start.5 = (f32[256,1024]{1,0:T(8,128)S(1)}, f32[256,1024]{1,0:T(8,128)}, u32[]{:S(2)}) copy-start(f32[256,1024]{1,0:T(8,128)} %copy-done.4) | copy-start | bytes 3145732
  118.1 29.6 %copy-start.6 = (bf16[64,2048]{1,0:T(8,128)(2,1)S(1)}, bf16[64,2048]{1,0:T(8,128)(2,1)}, u32[]{:S(2)}) copy-start(bf16[64,2048]{1,0:T(8,128)(2,1)} %param.13) | copy-start | bytes 786436

commit v2 on v1

--- a/solution.py
+++ b/solution.py
@@ -239,11 +239,19 @@
             + conv_weight[lower][None, :] * extended[lower : lower + seq_rows] * same_req[:, None]
         )
     activated = jax.nn.silu(conv_sum).astype(jnp.bfloat16)
-    x_part = jnp.dot(activated, w_x, preferred_element_type=jnp.float32)
-    x_proj = jnp.sum(exchange([x_part], [("chan", "gather")], 1)[0], axis=0)
-    thin_timescale_factor = x_proj[:, :rank_size].astype(jnp.bfloat16)
-    in_coef = x_proj[:, rank_size : rank_size + state_size]
-    out_coef = x_proj[:, rank_size + state_size :]
+    rank_part = jnp.dot(activated, w_x[:, :rank_size], preferred_element_type=jnp.float32)
+    coef_part = jnp.einsum(
+        "te,en->nt", activated, w_x[:, rank_size:], preferred_element_type=jnp.float32
+    )
+    rank_blocks, coef_blocks = exchange(
+        [rank_part.astype(jnp.bfloat16), coef_part.astype(jnp.bfloat16)],
+        [("chan", "gather"), ("chan", "gather")],
+        1,
+    )
+    thin_timescale_factor = jnp.sum(rank_blocks.astype(jnp.float32), axis=0).astype(jnp.bfloat16)
+    coef = jnp.sum(coef_blocks.astype(jnp.float32), axis=0).T
+    in_coef = coef[:, :state_size]
+    out_coef = coef[:, state_size:]
     timescale_values = position_presence[:, None] * jax.nn.softplus(
         jnp.dot(thin_timescale_factor, timescale_matrix, preferred_element_type=jnp.float32)
         + timescale_offset[None, :]

time: 149 us -> 139 us (0.933)
  Pallas kernels: 103 us -> 87.9 us
  local copies, waits for them, and re-layouts: 7.64 us -> 9.85 us
  other arithmetic: 19.7 us -> 21.4 us
    pallas_call x4, Pallas kernels: 91.5 us -> 76.7 us  [exchange(): pl.pallas_call(kernel, out_shape=out_shape, in_specs=[pl.BlockSpec(memory...]
    slice x1 -> x3, local copies, waits for them, and re-layouts: 0.76 us -> 2.83 us  [the longest x2 2.08 us: on_device(): out_coef = coef[:, state_size:]]
where the time goes in v2:
time: 139 us; the launch traced here: 138 us
  Pallas kernels  87.9 us (63%)
  other arithmetic  21.4 us (15%)
  matrix products  14.6 us (11%)
  local copies, waits for them, and re-layouts  9.85 us (7%)
  starting transfers between devices  3.5 us (3%)
    pallas_call x4, Pallas kernels, exchange(): pl.pallas_call(kernel, out_shape=out_shape, in_specs=[pl.BlockSpec(memory...  76.7 us
    pallas_call x2, Pallas kernels, run_scan(): pl.pallas_call(kernel, out_shape=out_shape, in_specs=[smem] + [vmem] * (l...  11.2 us
    dot_general x1, matrix products, on_device(): jnp.einsum('td,kde->kte', exchange([rescaled_entries], [('chan', 'gather'...  6.07 us
    select_n x1, other arithmetic, on_device(): jnp.where(span < me, onward + span_ends[span, :state_size], incoming)  5.7 us
    dot_general x1, matrix products, on_device(): jnp.dot(switched_result, w_out, preferred_element_type=jnp.float32)  4.98 us
    ppermute x1, starting transfers between devices, shifted(): return lax.ppermute(block, axis, route)  3.5 us
  transfers between devices with their start and end apart: 1, of which 0 were waited for; matrix products, arithmetic and copies ran while one was open for 2% of the time, Pallas kernels for 0%

profile of v2, /device:TPU:9, one launch (start us, length us, event | category | flops | bytes accessed | tf_op | source)
XLA Modules:
  0.0 138.3 jit_solution(557916468704066210)
XLA Ops:
  2.4 0.9 select_reduce_fusion.3
  3.4 1.1 fusion.17
  4.5 1.8 %fusion.19.refs_0_ = bf16[64,2048]{1,0:T(8,128)(2,1)} fusion(bf16[64,2048]{1,0:T(8,128)(2,1)} %param.13, f32[2048]{0:T(1024)} %param.14, f32[64]{0:T(128)S(1)} %add_rsqrt_fusion), kind=kLoop, calls=%fused_computation.43 | loop fusion | flops 524288 | bytes 532736 | tf_op jit(solution)/shard_map/convert_element_type | solution.py:220
  6.3 26.5 %shard_map.148 = bf16[4,64,2048]{2,1,0:T(8,128)(2,1)} custom-call(bf16[64,2048]{1,0:T(8,128)(2,1)} %fusion.19.refs_0_), custom_call_target="tpu_custom_call" | custom-call | tf_op jit(solution)/shard_map/pallas_call | solution.py:93
  32.9 6.1 %convolution_bitcast_fusion = f32[2,256,1024]{2,1,0:T(8,128)S(1)} fusion(bf16[256,2048,1]{1,0,2:T(8,128)(2,1)} %bitcast.81, bf16[2,2048,1024]{2,1,0:T(8,128)(2,1)} %param.15), kind=kOutput, calls=%fused_computation.3 | convolution fusion | flops 2147483648 | bytes 11534336 | tf_op jit(solution)/shard_map/td,kde->kte/dot_general | solution.py:221
  39.1 3.5 %collective-permute-start = (bf16[3,1024]{1,0:T(4,128)(2,1)S(1)}, bf16[3,1024]{1,0:T(4,128)(2,1)S(1)}, u32[]{:S(2)}, u32[]{:S(2)}) collective-permute-start(bf16[3,1024]{1,0:T(4,128)(2,1)S(1)} %slice.205), channel_id=1, source_target_pairs={{0,4},{4,8},{8,12},{12,16},{16,20},{20,24},{24,28},{1,5},{5,9},{9,... | collective-permute-start | bytes 18440 | tf_op jit(solution)/shard_map/ppermute | solution.py:14
  44.3 0.9 fusion.22
  46.1 0.9 multiply_convert_fusion.1
  47.1 0.9 convolution_convert_fusion.1.refs_0_
  48.0 0.9 fusion.refs_1_
  48.9 9.6 %shard_map.149 = (bf16[4,256,128]{2,1,0:T(8,128)(2,1)}, bf16[4,32,256]{2,1,0:T(8,128)(2,1)}) custom-call(bf16[256,128]{1,0:T(8,128)(2,1)} %convolution_convert_fusion.1.refs_0_, bf16[32,256]{1,0:T(8,128)(2,1)} %fusion.refs_1_), custom_call_target="tpu_custom_call" | custom-call | tf_op jit(solution)/shard_map/pallas_call | solution.py:93
  60.8 1.0 reduce_sum.197
  63.7 4.2 %shard_map.150.refs_0_ = f32[24,1024]{1,0:T(8,128)S(1)} custom-call(f32[4]{0:T(128)S(1)} %select_reduce_fusion.2.refs_0_, f32[256,1024]{1,0:T(8,128)S(1)} %get-tuple-element.45.refs_1_, f32[256,1024]{1,0:T(8,128)S(1)} %get-tuple-element.44.refs_2_, f32[16,1024]{1,0:T(8,128)S(1)} %exponential_negate_fusion.refs_3_, f32[256,16,128]{2,1,0:T(8,128)S(1)} %broadcast_in_dim.48.refs_4_), custom_call_target="tpu_custom_call" | custom-call | tf_op jit(solution)/shard_map/pallas_call | solution.py:180
  68.5 14.1 %shard_map.151 = f32[8,24,1024]{2,1,0:T(8,128)} custom-call(f32[24,1024]{1,0:T(8,128)} %copy-done.3), custom_call_target="tpu_custom_call" | custom-call | tf_op jit(solution)/shard_map/pallas_call | solution.py:93
  82.6 1.5 %slice_reduce_fusion.6 = (f32[1024]{0:T(1024)S(1)}, f32[1024]{0:T(1024)S(1)}, f32[1024]{0:T(1024)S(1)}, f32[1024]{0:T(1024)}, f32[1024]{0:T(1024)}, /*index=5*/f32[1024]{0:T(1024)}, f32[1024]{0:T(1024)}) fusion(f32[8,24,1024]{2,1,0:T(8,128)} %shard_map.151), kind=kLoop, calls=%fused_computation.78 | loop fusion | flops 50176 | bytes 258048 | tf_op jit(solution)/shard_map/reduce_sum | solution.py:280
  84.1 1.5 %copy.23 = f32[256,16]{1,0:T(8,128)} copy(f32[256,16]{0,1:T(8,128)} %get-tuple-element.33) | data formatting | bytes 32768 | tf_op jit(solution)/shard_map/slice | solution.py:254
  85.6 5.7 %fusion.31.refs_6_ = f32[16,1024]{1,0:T(8,128)S(1)} fusion(f32[8,24,1024]{2,1,0:T(8,128)} %shard_map.151, f32[1024]{0:T(1024)S(1)} %get-tuple-element.16, f32[]{:T(128)} %get-tuple-element.27, f32[1024]{0:T(1024)S(1)} %get-tuple-element.17, f32[]{:T(128)} %get-tuple-element.28, f32[1024]{0:T(1024)} %get-tuple-element.18, f32[]{:T(128)} %get-tuple-element.29, ...), kind=kLoop, calls=%fused_computation.57 | loop fusion | flops 589824 | bytes 618531 | tf_op jit(solution)/shard_map/jit(_where)/select_n | solution.py:282
  91.3 1.5 %broadcast_in_dim.49.refs_5_ = f32[256,16,128]{2,1,0:T(8,128)S(1)} broadcast(f32[256,16]{1,0:T(8,128)} %copy.23), dimensions={0,1} | broadcast | bytes 2113536 | tf_op jit(solution)/shard_map/broadcast_in_dim | solution.py:275
  92.9 7.0 %shard_map.152 = (f32[256,1024]{1,0:T(8,128)S(1)}, f32[4,16,1024]{2,1,0:T(8,128)S(1)}) custom-call(f32[4]{0:T(128)S(1)} %select_reduce_fusion.2.refs_0_, f32[256,1024]{1,0:T(8,128)S(1)} %copy-done.2, f32[256,1024]{1,0:T(8,128)S(1)} %get-tuple-element.44.refs_2_, f32[16,1024]{1,0:T(8,128)S(1)} %exponential_negate_fusion.refs_3_, ...), custom_call_target="tpu_custom_call" | custom-call | tf_op jit(solution)/shard_map/pallas_call | solution.py:180
  99.9 1.0 copy-done.4
  102.4 5.0 %convolution_convert_fusion = bf16[256,2048]{1,0:T(8,128)(2,1)} fusion(bf16[1024,2048]{1,0:T(8,128)(2,1)} %param.23, f32[256,1024]{1,0:T(8,128)S(1)} %copy-done.5, bf16[256,1024]{1,0:T(8,128)(2,1)S(1)} %copy-done.9, f32[2,256,1024]{2,1,0:T(8,128)} %copy-done.7, f32[1024]{0:T(1024)S(1)} %copy-done.20, f32[256]{0:T(256)S(1)} %copy-done.16), kind=kOutput, calls=%fused_computation.1 | convolution fusion | flops 1077149696 | bytes 7345152 | tf_op jit(solution)/shard_map/dot_general | solution.py:292
  107.4 26.4 %shard_map.153 = (bf16[4,64,2048]{2,1,0:T(8,128)(2,1)}, f32[8,80,128]{2,1,0:T(8,128)}) custom-call(bf16[4,64,2048]{2,1,0:T(8,128)(2,1)} %bitcast.82, f32[8,80,128]{2,1,0:T(8,128)} %bitcast.80), custom_call_target="tpu_custom_call" | custom-call | tf_op jit(solution)/shard_map/pallas_call | solution.py:93
  133.8 1.0 reduce_sum.209
  136.1 1.4 %convert_reduce_fusion = f32[64,2048]{1,0:T(8,128)S(1)} fusion(bf16[4,64,2048]{2,1,0:T(8,128)(2,1)} %get-tuple-element.13), kind=kLoop, calls=%fused_computation.2 | loop fusion | flops 917504 | bytes 1572864 | tf_op jit(solution)/shard_map/reduce_sum | solution.py:313
  (89 shorter events, 12.9 us)
Async XLA Ops:
  0.6 61.2 %copy-start = (bf16[128,1024]{1,0:T(8,128)(2,1)S(1)}, bf16[128,1024]{1,0:T(8,128)(2,1)}, u32[]{:S(2)}) copy-start(bf16[128,1024]{1,0:T(8,128)(2,1)} %param.19) | copy-start | bytes 786436
  3.4 58.3 %copy-start.15 = (f32[256]{0:T(256)}, f32[256]{0:T(256)S(1)}, u32[]{:S(2)}) copy-start(f32[256]{0:T(256)S(1)} %slice_convert_fusion.2) | copy-start | bytes 3076
  32.9 10.4 %copy-start.13 = (f32[4,1024]{1,0:T(4,128)S(1)}, f32[4,1024]{1,0:T(4,128)}, u32[]{:S(2)}) copy-start(f32[4,1024]{1,0:T(4,128)} %param.16) | copy-start | bytes 49156
  32.9 10.6 %copy-start.11 = (f32[16,1024]{1,0:T(8,128)S(1)}, f32[16,1024]{1,0:T(8,128)}, u32[]{:S(2)}) copy-start(f32[16,1024]{1,0:T(8,128)} %param.21) | copy-start | bytes 196612
  39.0 7.1 %copy-start.7 = (f32[2,256,1024]{2,1,0:T(8,128)}, f32[2,256,1024]{2,1,0:T(8,128)S(1)}, u32[]{:S(2)}) copy-start(f32[2,256,1024]{2,1,0:T(8,128)S(1)} %convolution_bitcast_fusion) | copy-start | bytes 6291460
  39.0 7.1 %copy-start.18 = (f32[1024]{0:T(1024)S(1)}, f32[1024]{0:T(1024)}, u32[]{:S(2)}) copy-start(f32[1024]{0:T(1024)} %param.17) | copy-start | bytes 12292
  39.1 6.8 %collective-permute-start = (bf16[3,1024]{1,0:T(4,128)(2,1)S(1)}, bf16[3,1024]{1,0:T(4,128)(2,1)S(1)}, u32[]{:S(2)}, u32[]{:S(2)}) collective-permute-start(bf16[3,1024]{1,0:T(4,128)(2,1)S(1)} %slice.205), channel_id=1, source_target_pairs={{0,4},{4,8},{8,12},{12,16},{16,20},{20,24},{24,28},{1,5},{5,9},{9,... | collective-permute-start | bytes 18440 | tf_op jit(solution)/shard_map/ppermute | solution.py:14
  46.1 1.0 copy-start.14
  47.1 14.7 %copy-start.8 = (bf16[256,1024]{1,0:T(8,128)(2,1)}, bf16[256,1024]{1,0:T(8,128)(2,1)S(1)}, u32[]{:S(2)}) copy-start(bf16[256,1024]{1,0:T(8,128)(2,1)S(1)} %multiply_convert_fusion.1) | copy-start | bytes 1572868
  47.1 14.7 %copy-start.19 = (f32[1024]{0:T(1024)S(1)}, f32[1024]{0:T(1024)}, u32[]{:S(2)}) copy-start(f32[1024]{0:T(1024)} %param.20) | copy-start | bytes 12292
  61.8 0.9 copy-start.10
  62.7 1.0 copy-start.1
  67.9 0.6 copy-start.3
  85.6 7.2 %copy-start.2 = (f32[256,1024]{1,0:T(8,128)S(1)}, f32[256,1024]{1,0:T(8,128)}, u32[]{:S(2)}) copy-start(f32[256,1024]{1,0:T(8,128)} %copy-done.1) | copy-start | bytes 3145732
  92.8 8.1 %copy-start.17 = (f32[4,4]{1,0:T(4,128)S(1)}, f32[4,4]{1,0:T(4,128)}, u32[]{:S(2)}) copy-start(f32[4,4]{1,0:T(4,128)} %compare_convert_fusion) | copy-start | bytes 196
  92.8 8.2 %copy-start.12 = (f32[4,4,1024]{2,1,0:T(4,128)S(1)}, f32[4,4,1024]{2,1,0:T(4,128)}, u32[]{:S(2)}) copy-start(f32[4,4,1024]{2,1,0:T(4,128)} %fusion.22) | copy-start | bytes 196612
  99.9 1.0 copy-start.4
  100.9 1.1 copy-start.9
  100.9 1.1 copy-start.16
  100.9 1.1 copy-start.20
  100.9 1.5 %copy-start.5 = (f32[256,1024]{1,0:T(8,128)S(1)}, f32[256,1024]{1,0:T(8,128)}, u32[]{:S(2)}) copy-start(f32[256,1024]{1,0:T(8,128)} %copy-done.4) | copy-start | bytes 3145732
  107.4 30.1 %copy-start.6 = (bf16[64,2048]{1,0:T(8,128)(2,1)S(1)}, bf16[64,2048]{1,0:T(8,128)(2,1)}, u32[]{:S(2)}) copy-start(bf16[64,2048]{1,0:T(8,128)(2,1)} %param.13) | copy-start | bytes 786436
